TPU v7x, 32 devices: a whole 2x2x4 slice. The times are simulated.
32 devices in a mesh: col: 16 (over z, x, core), row: 2 (over y).
Axes of the slice: x: 2, y: 2, z: 4, core: 2. Of those that a mesh axis runs over, the one named last changes fastest.
Arguments:
- covering_tiles: bfloat16 [2, 1024, 128, 128], P('row', 'col'), may hold values from -0.09375 to 0.09375
- tile_row_blocks: int32 [2, 1024], P('row', 'col'), may hold values from 0 to 31
- tile_cols: int32 [2, 1024], P('row', 'col'), may hold values from 0 to 63
- cut_tiles: bfloat16 [16, 128, 128, 128], P('col', 'row'), may hold values from -0.0625 to 0.0625
- cut_dest: int32 [16, 128, 1], P('col', 'row'), may hold values from 0 to 15; in each aligned block of 64 rows (0 to 63, 64 to 127, ..., all dimensions but the last counted through in order) at most 8 rows name the same one
- cut_cols: int32 [16, 128], P('col', 'row'), may hold values from 0 to 63
- cost: float32 [1024, 128], P('col'), may hold values from -30 to 30
- demand: float32 [64, 128], P('row'), may hold values from 0 to 12
- primal_start: float32 [1024, 128], P('col'), may hold values from 0 to 1
- initial_duals: float32 [64, 128], P('row'), may hold values from 0 to 1
- cut_start: float32 [16, 256], P('col', 'row'), may hold values from 0 to 1
- primal_weight: float32 [1], replicated, may hold values from 0.5 to 2
- step_size: float32 [1], replicated, may hold values from 0.3 to 0.6
- exponents: int32 [1024], P('col'), may hold values from 0 to 3
Outputs:
- primal: float32 [1024, 128], P('col')
- dual: float32 [64, 128], P('row')
- cut_dual: float32 [16, 256], P('col', 'row')
- violation: float32 [1024, 128], P('col')
Inputs may be any that keep to these rules, and one draw needn't show every extreme that they name: `cut_dest`: the cut tiles of one device touch at most 8 times the same column shard; some device reaches 8.
All inputs are finite; a program needn't handle non-finite values.
Results may differ from a plain program's by a relative error of at most 0.0017.
The roundings to bfloat16 on the way count: a program that leaves them out, or rounds other values in their place, can miss the bound.
Values may be sent and summed in bfloat16 or wider, within the bound.
A program may use at most 64 MiB of HBM per device.

v0:
```python
import jax
import jax.numpy as jnp
from jax import lax
from jax.sharding import PartitionSpec as P

ITERS = 2


EPSILON = 1e-06


def one_hot_rows(index, tally_number):
    return (index[:, None] == jnp.arange(tally_number, dtype=jnp.int32)[None, :]).astype(
        jnp.float32
    )


def spread_onto(table, values):
    return jnp.einsum(
        "kn,kb->nb",
        table,
        values,
        precision=lax.Precision.HIGHEST,
        preferred_element_type=jnp.float32,
    )


def local(
    covering_tiles,
    tile_row_blocks,
    tile_cols,
    cut_tiles,
    cut_dest,
    cut_cols,
    cost,
    demand,
    primal_start,
    initial_duals,
    cut_start,
    primal_weight,
    step_size,
    exponents,
):
    tiles = covering_tiles[0]
    rows_here = tile_row_blocks[0]
    cols_here = tile_cols[0]
    cuts = cut_tiles[0]
    target = cut_dest[0, :, 0]
    cut_block = cut_cols[0]
    blocks = cost.shape[0]
    width = cost.shape[1]
    row_blocks = demand.shape[0]
    owners = lax.axis_size("col")
    cut_count = cuts.shape[0]
    capacity = max(2, (2 * cut_count + owners - 1) // owners)
    slots = owners * capacity
    match = (target[:, None] == jnp.arange(owners, dtype=jnp.int32)[None, :]).astype(jnp.int32)
    before = jnp.cumsum(match, axis=0) - match
    rank = jnp.sum(before * match, axis=1)
    slot = target * capacity + rank
    wanted = jnp.full((slots,), blocks, jnp.int32).at[slot].set(cut_block)
    row_table = one_hot_rows(rows_here, row_blocks)
    col_table = one_hot_rows(cols_here, blocks)

    def column_partial(ybar):
        entry_values = jnp.einsum(
            "tij,ti->tj", tiles, ybar[rows_here], preferred_element_type=jnp.float32
        )
        return spread_onto(col_table, entry_values)

    send_tiles = jnp.zeros((slots, width, width), jnp.bfloat16).at[slot].set(cuts)
    held, held_block = (
        lax.all_to_all(send_tiles, "col", split_axis=0, concat_axis=0, tiled=True),
        lax.all_to_all(wanted, "col", split_axis=0, concat_axis=0, tiled=True),
    )
    held_table = one_hot_rows(held_block, blocks)
    safe_block = jnp.minimum(held_block, blocks - 1)

    def cut_price(wbar):
        every = lax.all_gather(wbar, "col", axis=0, tiled=True)
        per_slot = jnp.repeat(every, capacity, axis=0)
        entry_values = jnp.einsum("kij,ki->kj", held, per_slot, preferred_element_type=jnp.float32)
        return spread_onto(held_table, entry_values)

    def gradient(dual, cut_dual):
        partial_value = cut_price(cut_dual.astype(jnp.bfloat16)) - column_partial(
            dual.astype(jnp.bfloat16)
        )
        return cost + lax.psum(partial_value, "row")

    eta = step_size[0]
    omega = primal_weight[0]
    primal = primal_start
    dual = initial_duals
    cut_dual = cut_start
    for turn in range(ITERS):
        grad = gradient(dual, cut_dual)
        tau = eta / omega
        sigma = eta * omega
        new_primal = jnp.clip(primal - tau * grad, 0.0, 1.0)
        xbar = (2.0 * new_primal - primal).astype(jnp.bfloat16)
        row_entry_values = jnp.einsum(
            "tij,tj->ti", tiles, xbar[cols_here], preferred_element_type=jnp.float32
        )
        partial_value = spread_onto(row_table, row_entry_values)
        total = lax.psum(partial_value, "col")
        new_dual = jnp.maximum(dual + sigma * (demand - total), 0.0)
        step_y = new_dual - dual
        dual_term = jnp.sum(step_y * step_y) / owners
        cut_entry_values = jnp.einsum(
            "kij,kj->ki", held, xbar[safe_block], preferred_element_type=jnp.float32
        )
        back = lax.all_to_all(cut_entry_values, "col", split_axis=0, concat_axis=0, tiled=True)
        new_cut = jnp.maximum(cut_dual + sigma * (jnp.sum(back[slot], axis=0)[None, :] - 1.0), 0.0)
        if turn + 1 < ITERS:
            step_x = new_primal - primal
            step_w = new_cut - cut_dual
            primal_term = jnp.sum(step_x * step_x)
            dual_term = dual_term + jnp.sum(step_w * step_w)
            moved = lax.psum(primal_term, "col")
            dual_moved = lax.psum(dual_term, ("col", "row"))
            omega = jnp.sqrt(omega * jnp.sqrt((moved + EPSILON) / (dual_moved + EPSILON)))
        primal, dual, cut_dual = (new_primal, new_dual, new_cut)
    grad = gradient(dual, cut_dual)
    limit = (-0.125 * jnp.exp2(exponents.astype(jnp.float32)))[:, None]
    violation = jnp.maximum(limit - grad, 0.0)
    return (primal, dual, cut_dual, violation)


def solution(mesh):
    in_specs = (
        P("row", "col", None, None),
        P("row", "col"),
        P("row", "col"),
        P("col", "row", None, None),
        P("col", "row", None),
        P("col", "row"),
        P("col", None),
        P("row", None),
        P("col", None),
        P("row", None),
        P("col", "row"),
        P(),
        P(),
        P("col"),
    )
    out_specs = (P("col", None), P("row", None), P("col", "row"), P("col", None))
    return jax.shard_map(local, mesh=mesh, in_specs=in_specs, out_specs=out_specs, check_vma=False)
```

profile of v0, /device:TPU:0, one launch (start us, length us, event | category | flops | bytes accessed | tf_op | source)
XLA Modules:
  0.0 407.1 jit_solution(14927203985040006119)
XLA Ops:
  0.6 0.0 copy-start
  0.6 0.9 fusion.33
  1.5 0.1 reduce_window_sum.11
  1.6 0.8 select_reduce_fusion
  2.5 0.7 fusion.39
  3.1 0.9 scatter_custom_fusion
  4.0 0.7 all_to_all.25
  4.7 7.4 %all-to-all-start = ((s32[16,8,1]{1,2,0:T(1,128)}), s32[16,8,1]{1,2,0:T(1,128)S(1)}, u32[]{:S(2)}, u32[]{:S(2)}) async-start(s32[16,8,1]{1,2,0:T(1,128)} %bitcast.7), calls=%async_computation | async-start | bytes 16384 | tf_op jit(solution)/shard_map/all_to_all | solution.py:74
  12.1 3.0 broadcast_in_dim.8
  15.1 9.9 %scatter_fusion = bf16[128,128,128]{2,1,0:T(8,128)(2,1)} fusion(bf16[128,128,128]{2,1,0:T(8,128)(2,1)} %broadcast_in_dim.8, s32[64]{0:T(128)S(1)} %fusion.39, bf16[64,128,128]{2,1,0:T(8,128)(2,1)} %bitcast.128), kind=kCustom, calls=%fused_computation.10 | custom fusion | bytes 6291712 | tf_op jit(solution)/shard_map/scatter | solution.py:71
  25.1 0.0 copy-start.7
  25.1 6.2 %all-to-all-start.1 = ((bf16[128,128,128]{2,1,0:T(8,128)(2,1)}), bf16[128,128,128]{2,1,0:T(8,128)(2,1)}, u32[]{:S(2)}, u32[]{:S(2)}) async-start(bf16[128,128,128]{2,1,0:T(8,128)(2,1)} %scatter_fusion), calls=%async_computation.1 | async-start | bytes 8388608 | tf_op jit(solution)/shard_map/all_to_all | solution.py:73
  31.3 0.0 copy-start.1
  31.3 0.0 copy-start.2
  31.3 83.8 %all-gather = bf16[16,1,128]{2,1,0:T(2,128)(2,1)S(1)} all-gather(bf16[1,1,128]{2,1,0:T(2,128)(2,1)S(1)} %convert_bitcast_fusion.2), channel_id=1, replica_groups=mesh['col'=16,'row'=2] {'col'}, dimensions={0}, use_global_device_ids=true | all-gather | bytes 4352 | tf_op jit(solution)/shard_map/all_gather | solution.py:80
  116.5 0.6 gather_fusion
  117.3 0.6 fusion.8
  117.9 0.5 broadcast.214
  118.4 0.7 minimum_reduce_fusion
  119.1 0.1 eq.64
  119.2 0.1 min.32
  119.3 0.0 all-to-all-done.1
  119.4 3.4 fusion.18
  122.7 0.3 fusion.22
  123.0 0.3 convolution_subtract_fusion.2
  123.3 8.4 %psum.49 = f32[64,128]{1,0:T(8,128)S(1)} all-reduce(f32[64,128]{1,0:T(8,128)S(1)} %convolution_subtract_fusion.2), channel_id=1, replica_groups=mesh['col'=16,'row'=2] {'row'}, use_global_device_ids=true, to_apply=%region_4.5 | all-reduce | flops 8192 | bytes 65536 | tf_op jit(solution)/shard_map/psum | solution.py:89
  131.8 0.6 multiply_reduce_fusion
  132.4 0.6 gather_fusion.1
  133.0 1.2 fusion.6
  134.2 0.7 gather_fusion.2
  134.9 5.1 %fusion.16 = f32[128,1,128]{2,1,0:T(1,128)} fusion(bf16[128,128,128]{2,1,0:T(8,128)(2,1)} %all-to-all-done.1, bf16[128,128,1]{1,0,2:T(8,128)(2,1)S(1)} %bitcast.132), kind=kOutput, calls=%fused_computation.30 | convolution fusion | flops 4194304 | bytes 4292608 | tf_op jit(solution)/shard_map/kij,kj->ki/dot_general | solution.py:110
  140.0 22.8 %all-to-all-start.2 = ((f32[16,8,128]{2,1,0:T(8,128)}), f32[16,8,128]{2,1,0:T(8,128)S(1)}, u32[]{:S(2)}, u32[]{:S(2)}) async-start(f32[16,8,128]{2,1,0:T(8,128)} %bitcast.31), calls=%async_computation.2 | async-start | bytes 131072 | tf_op jit(solution)/shard_map/all_to_all | solution.py:113
  162.8 0.3 fusion.29
  163.0 61.9 %all-reduce = (f32[32,128]{1,0:T(8,128)S(1)}, f32[]{:T(128)}) all-reduce(f32[32,128]{1,0:T(8,128)S(1)} %fusion.29, f32[]{:T(128)} %get-tuple-element.18), channel_id=1, replica_groups=mesh['col'=16,'row'=2] {'col'}, use_global_device_ids=true, to_apply=%region_7.8 | all-reduce | flops 4097 | bytes 32776 | tf_op jit(solution)/shard_map/psum | solution.py:106
  224.9 0.6 multiply_reduce_fusion.1
  225.5 0.6 gather_fusion.4
  226.2 0.7 fusion.4
  227.5 0.6 gather_fusion.3
  228.1 0.6 multiply_reduce_fusion.2
  230.0 36.9 %psum.52 = f32[]{:T(128)} all-reduce(f32[]{:T(128)S(6)} %add.130), channel_id=1, replica_groups=mesh['col'=16,'row'=2] {'col','row'}, use_global_device_ids=true, to_apply=%region_11.12 | all-reduce | flops 1 | bytes 8 | tf_op jit(solution)/shard_map/psum | solution.py:121
  267.7 21.0 %all-gather.1 = bf16[16,1,128]{2,1,0:T(2,128)(2,1)S(1)} all-gather(bf16[1,1,128]{2,1,0:T(2,128)(2,1)S(1)} %convert_bitcast_fusion.1), channel_id=1, replica_groups=mesh['col'=16,'row'=2] {'col'}, dimensions={0}, use_global_device_ids=true | all-gather | bytes 4352 | tf_op jit(solution)/shard_map/all_gather | solution.py:80
  288.7 3.4 fusion.14
  292.1 0.3 fusion.21
  292.4 0.3 convolution_subtract_fusion.1
  292.7 7.5 %psum.53 = f32[64,128]{1,0:T(8,128)S(1)} all-reduce(f32[64,128]{1,0:T(8,128)S(1)} %convolution_subtract_fusion.1), channel_id=1, replica_groups=mesh['col'=16,'row'=2] {'row'}, use_global_device_ids=true, to_apply=%region_12.13 | all-reduce | flops 8192 | bytes 65536 | tf_op jit(solution)/shard_map/psum | solution.py:89
  300.3 0.6 subtract_convert_fusion
  300.9 0.7 gather_fusion.6
  301.6 0.6 gather_fusion.5
  302.3 5.1 %fusion.12 = f32[128,1,128]{2,1,0:T(1,128)} fusion(bf16[128,128,128]{2,1,0:T(8,128)(2,1)} %all-to-all-done.1, bf16[128,128,1]{1,0,2:T(8,128)(2,1)S(1)} %bitcast.131), kind=kOutput, calls=%fused_computation.26 | convolution fusion | flops 4194304 | bytes 4292608 | tf_op jit(solution)/shard_map/kij,kj->ki/dot_general | solution.py:110
  307.4 3.5 all-to-all-start.3
  310.9 1.2 fusion.2
  312.0 0.3 fusion.28
  312.3 61.9 %psum.54 = f32[32,128]{1,0:T(8,128)S(1)} all-reduce(f32[32,128]{1,0:T(8,128)S(1)} %fusion.28), channel_id=1, replica_groups=mesh['col'=16,'row'=2] {'col'}, use_global_device_ids=true, to_apply=%region_13.14 | all-reduce | flops 4096 | bytes 32768 | tf_op jit(solution)/shard_map/psum | solution.py:106
  374.2 0.6 fusion.47
  374.8 0.6 gather_fusion.8
  375.4 0.7 fusion
  376.1 0.6 gather_fusion.7
  376.7 0.5 convert_bitcast_fusion
  377.2 17.0 %all-gather.2 = bf16[16,1,128]{2,1,0:T(2,128)(2,1)S(1)} all-gather(bf16[1,1,128]{2,1,0:T(2,128)(2,1)S(1)} %get-tuple-element.10), channel_id=1, replica_groups=mesh['col'=16,'row'=2] {'col'}, dimensions={0}, use_global_device_ids=true | all-gather | bytes 4352 | tf_op jit(solution)/shard_map/all_gather | solution.py:80
  394.3 3.4 fusion.10
  397.6 0.3 fusion.20
  397.9 0.3 convolution_subtract_fusion
  398.2 8.2 %psum.55 = f32[64,128]{1,0:T(8,128)S(1)} all-reduce(f32[64,128]{1,0:T(8,128)S(1)} %convolution_subtract_fusion), channel_id=1, replica_groups=mesh['col'=16,'row'=2] {'row'}, use_global_device_ids=true, to_apply=%region_15.16 | all-reduce | flops 8192 | bytes 65536 | tf_op jit(solution)/shard_map/psum | solution.py:89
  406.4 0.7 subtract_maximum_fusion
  (38 shorter events, 0.2 us)
Async XLA Ops:
  0.6 116.6 %copy-start = (bf16[1,64,128,128]{3,2,1,0:T(8,128)(2,1)S(1)}, bf16[1,64,128,128]{3,2,1,0:T(8,128)(2,1)}, u32[]{:S(2)}) copy-start(bf16[1,64,128,128]{3,2,1,0:T(8,128)(2,1)} %param.14) | copy-start | bytes 6291460
  4.7 20.3 %all-to-all-start = ((s32[16,8,1]{1,2,0:T(1,128)}), s32[16,8,1]{1,2,0:T(1,128)S(1)}, u32[]{:S(2)}, u32[]{:S(2)}) async-start(s32[16,8,1]{1,2,0:T(1,128)} %bitcast.7), calls=%async_computation | async-start | bytes 16384 | tf_op jit(solution)/shard_map/all_to_all | solution.py:74
  25.0 6.2 %copy-start.6 = (f32[1,128]{1,0:T(1,128)S(1)}, f32[1,128]{1,0:T(1,128)}, u32[]{:S(2)}) copy-start(f32[1,128]{1,0:T(1,128)} %param.24) | copy-start | bytes 1540
  25.0 90.1 %copy-start.3 = (f32[32,128]{1,0:T(8,128)S(1)}, f32[32,128]{1,0:T(8,128)}, u32[]{:S(2)}) copy-start(f32[32,128]{1,0:T(8,128)} %param.23) | copy-start | bytes 49156
  25.0 91.4 %copy-start.8 = (s32[1,64]{1,0:T(1,128)S(1)}, s32[1,64]{1,0:T(1,128)}, u32[]{:S(2)}) copy-start(s32[1,64]{1,0:T(1,128)} %param.15) | copy-start | bytes 772
  25.1 92.1 %copy-start.5 = (s32[1,64]{1,0:T(1,128)S(1)}, s32[1,64]{1,0:T(1,128)}, u32[]{:S(2)}) copy-start(s32[1,64]{1,0:T(1,128)} %param.16) | copy-start | bytes 772
  25.1 92.2 %copy-start.7 = (s32[64]{0:T(128)S(1)}, s32[64]{0:T(128)}, u32[]{:S(2)}) copy-start(s32[64]{0:T(128)} %param.27) | copy-start | bytes 772
  25.1 94.3 %all-to-all-start.1 = ((bf16[128,128,128]{2,1,0:T(8,128)(2,1)}), bf16[128,128,128]{2,1,0:T(8,128)(2,1)}, u32[]{:S(2)}, u32[]{:S(2)}) async-start(bf16[128,128,128]{2,1,0:T(8,128)(2,1)} %scatter_fusion), calls=%async_computation.1 | async-start | bytes 8388608 | tf_op jit(solution)/shard_map/all_to_all | solution.py:73
  31.3 100.4 %copy-start.1 = (f32[64,128]{1,0:T(8,128)S(1)}, f32[64,128]{1,0:T(8,128)}, u32[]{:S(2)}) copy-start(f32[64,128]{1,0:T(8,128)} %param.20) | copy-start | bytes 98308
  31.3 100.4 %copy-start.2 = (f32[64,128]{1,0:T(8,128)S(1)}, f32[64,128]{1,0:T(8,128)}, u32[]{:S(2)}) copy-start(f32[64,128]{1,0:T(8,128)} %param.22) | copy-start | bytes 98308
  122.7 102.2 %copy-start.4 = (f32[32,128]{1,0:T(8,128)S(1)}, f32[32,128]{1,0:T(8,128)}, u32[]{:S(2)}) copy-start(f32[32,128]{1,0:T(8,128)} %param.21) | copy-start | bytes 49156
  140.0 87.5 %all-to-all-start.2 = ((f32[16,8,128]{2,1,0:T(8,128)}), f32[16,8,128]{2,1,0:T(8,128)S(1)}, u32[]{:S(2)}, u32[]{:S(2)}) async-start(f32[16,8,128]{2,1,0:T(8,128)} %bitcast.31), calls=%async_computation.2 | async-start | bytes 131072 | tf_op jit(solution)/shard_map/all_to_all | solution.py:113
  307.4 68.7 %all-to-all-start.3 = ((f32[16,8,128]{2,1,0:T(8,128)}), f32[16,8,128]{2,1,0:T(8,128)S(1)}, u32[]{:S(2)}, u32[]{:S(2)}) async-start(f32[16,8,128]{2,1,0:T(8,128)} %bitcast.48), calls=%async_computation.3 | async-start | bytes 131072 | tf_op jit(solution)/shard_map/all_to_all | solution.py:113
where the time goes:
time: 408 us; the launch traced here: 407 us
  blocking collectives  307 us (75%)
  starting transfers between devices  39.8 us (10%)
  matrix products  26.9 us (7%)
  local copies, waits for them, and re-layouts  21.1 us (5%)
  other arithmetic  7.57 us (2%)
  between operations  5.11 us (1%)
    psum x2, blocking collectives, local(): total = lax.psum(partial_value, 'col')  124 us
    all_gather x3, blocking collectives, cut_price(): every = lax.all_gather(wbar, 'col', axis=0, tiled=True)  122 us
    psum x1, blocking collectives, local(): dual_moved = lax.psum(dual_term, ('col', 'row'))  36.9 us
    all_to_all x2, starting transfers between devices, local(): lax.all_to_all(cut_entry_values, 'col', split_axis=0, concat_axis=0, tile...  26.3 us
    psum x3, blocking collectives, gradient(): return cost + lax.psum(partial_value, 'row')  24.1 us
    dot_general x2, matrix products, local(): jnp.einsum('kij,kj->ki', held, xbar[safe_block], preferred_element_type=j...  10.2 us
    dot_general x3, matrix products, cut_price(): jnp.einsum('kij,ki->kj', held, per_slot, preferred_element_type=jnp.float32)  10.1 us
    scatter x1, local copies, waits for them, and re-layouts, local(): jnp.zeros((slots, width, width), jnp.bfloat16).at[slot].set(cuts)  9.93 us
  transfers between devices with their start and end apart: 4, of which 0 were waited for; matrix products, arithmetic and copies ran while one was open for 5% of the time, Pallas kernels for 0%

commit v1 on v0

v1 whole, which is shorter than its diff:
```python
import functools

import jax
import jax.numpy as jnp
from jax import lax
from jax.experimental import pallas as pl
from jax.experimental.pallas import tpu as pltpu
from jax.sharding import PartitionSpec as P

ITERS = 2
EPSILON = 1e-06
GROUP = 16
STRIDE = 8
BF = jnp.bfloat16
F32 = jnp.float32
MESH = pl.DeviceIdType.MESH


def dot(a, b, contract):
    return lax.dot_general(a, b, ((contract[:1], contract[1:]), ((), ())), preferred_element_type=F32)


def split3(values):
    high = values.astype(BF)
    rest = values - high.astype(F32)
    middle = rest.astype(BF)
    low = (rest - middle.astype(F32)).astype(BF)
    return high, middle, low


def spread(table, values, contract):
    high, middle, low = split3(values)
    return dot(table, high, contract) + (dot(table, middle, contract) + dot(table, low, contract))


def kernel(
    owners,
    n_row,
    tiles,
    row_of,
    col_of,
    cuts,
    dest,
    cut_col,
    cost,
    demand,
    x0,
    y0,
    w0,
    weight,
    step,
    exps,
    x_out,
    y_out,
    w_out,
    v_out,
    send_a,
    recv_a,
    send_x,
    recv_x,
    send_p,
    recv_p,
    send_r,
    recv_r,
    sem_a,
    sem_x,
    sem_p,
    sem_r,
):
    c = lax.axis_index("col")
    r = lax.axis_index("row")
    n_dev = owners * n_row
    flat = r * owners + c
    count = tiles.shape[1]
    blocks, width = cost.shape
    row_blocks = demand.shape[0]
    slots = owners * STRIDE

    barrier = pltpu.get_barrier_semaphore()

    def greet(k, carry):
        other = lax.rem(flat + k, n_dev)
        pl.semaphore_signal(
            barrier,
            inc=1,
            device_id={"col": lax.rem(other, owners), "row": other // owners},
            device_id_type=MESH,
        )
        return carry

    lax.fori_loop(1, n_dev, greet, 0)

    def one_hot(row, size):
        return jnp.where(
            lax.broadcasted_iota(jnp.int32, (size, row.shape[1]), 0) == row, 1.0, 0.0
        )

    row_table = one_hot(row_of[...], row_blocks).astype(BF)
    col_table = one_hot(col_of[...], blocks).astype(BF)
    owner_table = one_hot(dest[...], max(owners, 16)).astype(BF)
    same = dot(owner_table, owner_table, (0, 0))
    earlier = lax.broadcasted_iota(jnp.int32, same.shape, 0) < lax.broadcasted_iota(
        jnp.int32, same.shape, 1
    )
    rank = jnp.sum(jnp.where(earlier, same, 0.0), axis=0, keepdims=True).astype(jnp.int32)
    slot_table = one_hot(dest[...] * STRIDE + rank, slots).astype(BF)
    block_table = one_hot(cut_col[...], width).astype(BF)
    chosen = dot(slot_table, block_table, (1, 1))

    line = lax.broadcasted_iota(jnp.int32, (GROUP, width), 0)
    masks = [jnp.where(line == k, 1.0, 0.0).astype(BF) for k in range(GROUP)]

    def forward(ref, rows_at):
        parts = []
        for g in range(count // GROUP):
            rows = rows_at(g)
            left = jnp.concatenate([rows * m for m in masks], axis=1)
            block = ref[0, g * GROUP : (g + 1) * GROUP].reshape(GROUP * width, width)
            parts.append(dot(left, block, (1, 0)))
        return jnp.concatenate(parts, axis=0)

    def backward(ref, vectors):
        parts = []
        for g in range(count // GROUP):
            rows = vectors[g * GROUP : (g + 1) * GROUP]
            total = jnp.zeros((GROUP, width), F32)
            for k in range(GROUP):
                total = total + dot(rows * masks[k], ref[0, g * GROUP + k], (1, 1))
            parts.append(total)
        return jnp.concatenate(parts, axis=0)

    def wait_all(buffer, number, sem):
        piece = buffer.at[pl.ds(0, number)]
        pltpu.make_async_copy(piece, piece, sem).wait()

    def send_cut(turn, w, stats):
        wb = jnp.broadcast_to(w, (GROUP, width)).astype(BF)
        products = forward(cuts, lambda g: wb)
        send_a[turn, :, :STRIDE] = spread(slot_table, products, (1, 0)).reshape(
            owners, STRIDE, width
        )
        send_a[turn, :, STRIDE:] = stats
        recv_a[turn, flat] = send_a[turn, c]

        def go(k, carry):
            other = lax.rem(flat + k, n_dev)
            oc, orow = lax.rem(other, owners), other // owners
            pltpu.make_async_remote_copy(
                src_ref=send_a.at[turn, oc],
                dst_ref=recv_a.at[turn, flat],
                send_sem=sem_a.at[0, turn],
                recv_sem=sem_a.at[1, turn],
                device_id={"col": oc, "row": orow},
                device_id_type=MESH,
            ).start()
            return carry

        lax.fori_loop(1, n_dev, go, 0)

    def send_rows(turn, y, moved):
        yg = dot(row_table, y.astype(BF), (0, 0)).astype(BF)
        products = forward(tiles, lambda g: yg[g * GROUP : (g + 1) * GROUP])
        send_r[turn, :blocks] = spread(col_table, products, (1, 0))
        send_r[turn, blocks:] = moved
        recv_r[turn, r] = send_r[turn]

        def go(k, carry):
            pltpu.make_async_remote_copy(
                src_ref=send_r.at[turn],
                dst_ref=recv_r.at[turn, r],
                send_sem=sem_r.at[0, turn],
                recv_sem=sem_r.at[1, turn],
                device_id={"col": c, "row": lax.rem(r + k, n_row)},
                device_id_type=MESH,
            ).start()
            return carry

        lax.fori_loop(1, n_row, go, 0)

    def to_columns(source, dest_ref, sems, turn):
        def go(k, carry):
            oc = lax.rem(c + k, owners)
            pltpu.make_async_remote_copy(
                src_ref=source(oc),
                dst_ref=dest_ref.at[turn, c],
                send_sem=sems.at[0, turn],
                recv_sem=sems.at[1, turn],
                device_id={"col": oc, "row": r},
                device_id_type=MESH,
            ).start()
            return carry

        lax.fori_loop(1, owners, go, 0)

    x, y, w = x0[...], y0[...], w0[...]
    pl.semaphore_wait(barrier, n_dev - 1)
    send_cut(0, w, chosen.reshape(owners, STRIDE, width))
    send_rows(0, y, jnp.zeros((STRIDE, width), F32))

    eta = jnp.full((1, 1), step[0], F32)
    omega = jnp.full((1, 1), weight[0], F32)
    held = None
    for turn in range(ITERS + 1):
        wait_all(recv_a.at[turn], n_dev - 1, sem_a.at[1, turn])
        if turn == 0:
            held = recv_a[0, :, STRIDE:].reshape(n_dev * STRIDE, width).astype(BF)
        prices = recv_a[turn, :, :STRIDE].reshape(n_dev * STRIDE, width)
        cut_part = spread(held, prices, (0, 0))[:blocks]
        wait_all(recv_r.at[turn], n_row - 1, sem_r.at[1, turn])
        from_rows = recv_r[turn, 0]
        for other in range(1, n_row):
            from_rows = from_rows + recv_r[turn, other]
        grad = cost[...] + (cut_part - from_rows[:blocks])
        if turn == 1:
            stats = jnp.sum(recv_a[turn, :, STRIDE:], axis=0)
            moved = jnp.sum(stats[:1], axis=1, keepdims=True)
            dual_moved = jnp.sum(
                stats[1:2] + jnp.sum(from_rows[blocks:], axis=0, keepdims=True),
                axis=1,
                keepdims=True,
            )
            omega = jnp.sqrt(omega * jnp.sqrt((moved + EPSILON) / (dual_moved + EPSILON)))
        if turn == ITERS:
            break
        tau = eta / omega
        sigma = eta * omega
        new_x = jnp.clip(x - tau * grad, 0.0, 1.0)
        xbar = (2.0 * new_x - x).astype(BF)

        mine = (
            recv_a[0, pl.ds(r * owners, owners), STRIDE:].reshape(slots, width)[:, :blocks].astype(BF)
        )
        send_x[turn] = dot(mine, xbar, (1, 0)).reshape(owners, STRIDE, width)
        recv_x[turn, c] = send_x[turn, c]
        to_columns(lambda oc: send_x.at[turn, oc], recv_x, sem_x, turn)

        xg = dot(col_table, xbar, (0, 0)).astype(BF)
        send_p[turn] = spread(row_table, backward(tiles, xg), (1, 0))
        recv_p[turn, c] = send_p[turn]
        to_columns(lambda oc: send_p.at[turn], recv_p, sem_p, turn)

        wait_all(recv_x.at[turn], owners - 1, sem_x.at[1, turn])
        xr = recv_x[turn].reshape(slots, width).astype(BF)
        xk = dot(slot_table, xr, (0, 0)).astype(BF)
        activity = jnp.sum(backward(cuts, xk), axis=0, keepdims=True)
        new_w = jnp.maximum(w + sigma * (activity - 1.0), 0.0)
        place = lax.broadcasted_iota(jnp.int32, (STRIDE, width), 0)
        step_x = jnp.where(r == 0, 1.0, 0.0) * (new_x - x)
        step_w = new_w - w
        stats = jnp.where(
            place == 0,
            jnp.sum(step_x * step_x, axis=0, keepdims=True),
            jnp.where(place == 1, step_w * step_w, 0.0),
        )
        send_cut(turn + 1, new_w, jnp.broadcast_to(stats[None], (owners, STRIDE, width)))

        wait_all(recv_p.at[turn], owners - 1, sem_p.at[1, turn])
        total = jnp.sum(recv_p[turn], axis=0)
        new_y = jnp.maximum(y + sigma * (demand[...] - total), 0.0)
        step_y = new_y - y
        squares = jnp.sum((step_y * step_y).reshape(row_blocks // STRIDE, STRIDE, width), axis=0)
        send_rows(turn + 1, new_y, squares)
        x, y, w = new_x, new_y, new_w

    x_out[...] = x
    y_out[...] = y
    w_out[...] = w
    here = lax.broadcasted_iota(jnp.int32, (blocks, blocks), 0) == lax.broadcasted_iota(
        jnp.int32, (blocks, blocks), 1
    )
    power = jnp.exp2(exps[...].astype(F32))
    limit = -0.125 * jnp.sum(jnp.where(here, power, 0.0), axis=1, keepdims=True)
    v_out[...] = jnp.maximum(limit - grad, 0.0)

    for turn in range(ITERS + 1):
        wait_all(recv_a.at[turn], n_dev - 1, sem_a.at[0, turn])
        wait_all(recv_r.at[turn], n_row - 1, sem_r.at[0, turn])
        if turn < ITERS:
            wait_all(recv_x.at[turn], owners - 1, sem_x.at[0, turn])
            wait_all(recv_p.at[turn], owners - 1, sem_p.at[0, turn])


def local(
    covering_tiles,
    tile_row_blocks,
    tile_cols,
    cut_tiles,
    cut_dest,
    cut_cols,
    cost,
    demand,
    primal_start,
    initial_duals,
    cut_start,
    primal_weight,
    step_size,
    exponents,
    owners,
    n_row,
):
    blocks, width = cost.shape
    row_blocks = demand.shape[0]
    n_dev = owners * n_row
    phases = ITERS + 1
    vmem = pl.BlockSpec(memory_space=pltpu.VMEM)
    smem = pl.BlockSpec(memory_space=pltpu.SMEM)
    return pl.pallas_call(
        functools.partial(kernel, owners, n_row),
        out_shape=(
            jax.ShapeDtypeStruct(primal_start.shape, F32),
            jax.ShapeDtypeStruct(initial_duals.shape, F32),
            jax.ShapeDtypeStruct(cut_start.shape, F32),
            jax.ShapeDtypeStruct(cost.shape, F32),
        ),
        in_specs=[vmem] * 11 + [smem] * 2 + [vmem],
        out_specs=(vmem,) * 4,
        scratch_shapes=[
            pltpu.VMEM((phases, owners, 2 * STRIDE, width), F32),
            pltpu.VMEM((phases, n_dev, 2 * STRIDE, width), F32),
            pltpu.VMEM((ITERS, owners, STRIDE, width), F32),
            pltpu.VMEM((ITERS, owners, STRIDE, width), F32),
            pltpu.VMEM((ITERS, row_blocks, width), F32),
            pltpu.VMEM((ITERS, owners, row_blocks, width), F32),
            pltpu.VMEM((phases, blocks + STRIDE, width), F32),
            pltpu.VMEM((phases, n_row, blocks + STRIDE, width), F32),
            pltpu.SemaphoreType.DMA((2, phases)),
            pltpu.SemaphoreType.DMA((2, ITERS)),
            pltpu.SemaphoreType.DMA((2, ITERS)),
            pltpu.SemaphoreType.DMA((2, phases)),
        ],
        compiler_params=pltpu.CompilerParams(
            collective_id=0, has_side_effects=True, vmem_limit_bytes=44 * 1024 * 1024
        ),
        name="pdhg",
    )(
        covering_tiles,
        tile_row_blocks,
        tile_cols,
        cut_tiles,
        cut_dest.reshape(cut_cols.shape),
        cut_cols,
        cost,
        demand,
        primal_start,
        initial_duals,
        cut_start,
        primal_weight,
        step_size,
        exponents.reshape(1, blocks),
    )


def solution(mesh):
    in_specs = (
        P("row", "col", None, None),
        P("row", "col"),
        P("row", "col"),
        P("col", "row", None, None),
        P("col", "row", None),
        P("col", "row"),
        P("col", None),
        P("row", None),
        P("col", None),
        P("row", None),
        P("col", "row"),
        P(),
        P(),
        P("col"),
    )
    out_specs = (P("col", None), P("row", None), P("col", "row"), P("col", None))
    body = functools.partial(local, owners=mesh.shape["col"], n_row=mesh.shape["row"])
    return jax.shard_map(body, mesh=mesh, in_specs=in_specs, out_specs=out_specs, check_vma=False)
```

time: 408 us -> 61.2 us (0.15)
  blocking collectives: 307 us -> 0 us
  Pallas kernels: 0 us -> 46.3 us
  starting transfers between devices: 39.8 us -> 0 us
  matrix products: 26.9 us -> 0 us
  local copies, waits for them, and re-layouts: 21.1 us -> 12.4 us
  other arithmetic: 7.57 us -> 0 us
    psum x6 -> x0, blocking collectives: 185 us -> none  [the longest x2 124 us: local(): total = lax.psum(partial_value, 'col')]
    all_gather x3 -> x0, blocking collectives: 122 us -> none  [cut_price(): every = lax.all_gather(wbar, 'col', axis=0, tiled=True)]
    pallas_call x0 -> x1, Pallas kernels: none -> 46.3 us  [local(): pl.pallas_call(functools.partial(kernel, owners, n_row), out_shape=(jax.S...]
    all_to_all x4 -> x0, starting transfers between devices: 39.8 us -> none  [the longest x2 26.3 us: local(): lax.all_to_all(cut_entry_values, 'col', split_axis=0, concat_axis=0, tile...]
    dot_general x18 -> x0, matrix products: 26.9 us -> none  [the longest x2 10.2 us: local(): jnp.einsum('kij,kj->ki', held, xbar[safe_block], preferred_element_type=j...]
    unnamed x21 -> x28, local copies, waits for them, and re-layouts: 0.06 us -> 12.4 us
    scatter x2 -> x0, local copies, waits for them, and re-layouts: 10.8 us -> none  [the longest x1 9.93 us: local(): jnp.zeros((slots, width, width), jnp.bfloat16).at[slot].set(cuts)]
    gather x9 -> x0, local copies, waits for them, and re-layouts: 5.82 us -> none  [the longest x3 1.91 us: column_partial(): ybar[rows_here]]
  transfers between devices with their start and end apart: 4 -> 0, of which waited for: 0 -> 0; matrix products, arithmetic and copies ran while one was open for 5% -> 0% of each run, Pallas kernels for 0% -> 0%
where the time goes in v1:
time: 61.2 us; the launch traced here: 60.7 us
  Pallas kernels  46.3 us (76%)
  local copies, waits for them, and re-layouts  12.4 us (20%)
  between operations  1.96 us (3%)
    pallas_call x1, Pallas kernels, local(): pl.pallas_call(functools.partial(kernel, owners, n_row), out_shape=(jax.S...  46.3 us
    unnamed x28, local copies, waits for them, and re-layouts  12.4 us

profile of v1, /device:TPU:0, one launch (start us, length us, event | category | flops | bytes accessed | tf_op | source)
XLA Modules:
  0.0 60.7 jit_solution(15355170731429421154)
XLA Ops:
  1.9 0.0 copy-start
  1.9 1.6 %copy-done = bf16[1,64,128,128]{3,2,1,0:T(8,128)(2,1)S(1)} copy-done((bf16[1,64,128,128]{3,2,1,0:T(8,128)(2,1)S(1)}, bf16[1,64,128,128]{3,2,1,0:T(8,128)(2,1)}, u32[]{:S(2)}) %copy-start) | copy-done | bytes 2097176
  3.5 0.0 copy-start.1
  3.5 1.6 %copy-done.1 = bf16[1,64,128,128]{3,2,1,0:T(8,128)(2,1)S(1)} copy-done((bf16[1,64,128,128]{3,2,1,0:T(8,128)(2,1)S(1)}, bf16[1,64,128,128]{3,2,1,0:T(8,128)(2,1)}, u32[]{:S(2)}) %copy-start.1) | copy-done | bytes 2097176
  5.1 0.0 copy-start.2
  5.1 0.8 %copy-done.2 = f32[64,128]{1,0:T(8,128)S(1)} copy-done((f32[64,128]{1,0:T(8,128)S(1)}, f32[64,128]{1,0:T(8,128)}, u32[]{:S(2)}) %copy-start.2) | copy-done | bytes 32792
  5.9 0.0 copy-start.3
  5.9 0.8 %copy-done.3 = f32[64,128]{1,0:T(8,128)S(1)} copy-done((f32[64,128]{1,0:T(8,128)S(1)}, f32[64,128]{1,0:T(8,128)}, u32[]{:S(2)}) %copy-start.3) | copy-done | bytes 32792
  6.6 0.0 copy-start.4
  6.6 0.7 %copy-done.4 = f32[32,128]{1,0:T(8,128)S(1)} copy-done((f32[32,128]{1,0:T(8,128)S(1)}, f32[32,128]{1,0:T(8,128)}, u32[]{:S(2)}) %copy-start.4) | copy-done | bytes 16408
  7.3 0.0 copy-start.5
  7.3 0.7 %copy-done.5 = f32[32,128]{1,0:T(8,128)S(1)} copy-done((f32[32,128]{1,0:T(8,128)S(1)}, f32[32,128]{1,0:T(8,128)}, u32[]{:S(2)}) %copy-start.5) | copy-done | bytes 16408
  8.1 0.0 copy-start.6
  8.1 0.7 %copy-done.6 = s32[1,64]{1,0:T(1,128)S(1)} copy-done((s32[1,64]{1,0:T(1,128)S(1)}, s32[1,64]{1,0:T(1,128)}, u32[]{:S(2)}) %copy-start.6) | copy-done | bytes 280
  8.7 0.0 copy-start.7
  8.7 0.7 %copy-done.7 = s32[1,64]{1,0:T(1,128)S(1)} copy-done((s32[1,64]{1,0:T(1,128)S(1)}, s32[1,64]{1,0:T(1,128)}, u32[]{:S(2)}) %copy-start.7) | copy-done | bytes 280
  9.4 0.0 copy-start.8
  9.4 0.7 %copy-done.8 = s32[1,64,1]{1,2,0:T(1,128)S(1)} copy-done((s32[1,64,1]{1,2,0:T(1,128)S(1)}, s32[1,64,1]{1,2,0:T(1,128)}, u32[]{:S(2)}) %copy-start.8) | copy-done | bytes 280
  10.0 0.0 copy-start.9
  10.0 0.7 %copy-done.9 = s32[1,64]{1,0:T(1,128)S(1)} copy-done((s32[1,64]{1,0:T(1,128)S(1)}, s32[1,64]{1,0:T(1,128)}, u32[]{:S(2)}) %copy-start.9) | copy-done | bytes 280
  10.7 0.0 copy-start.10
  10.7 0.7 %copy-done.10 = f32[1,128]{1,0:T(1,128)S(1)} copy-done((f32[1,128]{1,0:T(1,128)S(1)}, f32[1,128]{1,0:T(1,128)}, u32[]{:S(2)}) %copy-start.10) | copy-done | bytes 536
  11.3 0.0 copy-start.11
  11.3 0.7 %copy-done.11 = s32[64]{0:T(128)S(1)} copy-done((s32[64]{0:T(128)S(1)}, s32[64]{0:T(128)}, u32[]{:S(2)}) %copy-start.11) | copy-done | bytes 280
  12.0 46.3 %pdhg.1 = (f32[64,128]{1,0:T(8,128)S(1)}, f32[32,128]{1,0:T(8,128)S(1)}, f32[1,128]{1,0:T(1,128)S(1)}, f32[64,128]{1,0:T(8,128)S(1)}) custom-call(bf16[1,64,128,128]{3,2,1,0:T(8,128)(2,1)S(1)} %copy-done, s32[1,64]{1,0:T(1,128)S(1)} %copy-done.6, s32[1,64]{1,0:T(1,128)S(1)} %copy-done.7, bf16[1,64,128,128]{3,2,1,0:T(8,128)(2,1)S(1)} %copy-done.1, ...), custom_call_target="tpu_custom_call" | custom-call | tf_op jit(solution)/shard_map/pdhg/pallas_call | solution.py:307
  58.3 0.6 %copy.24 = f32[64,128]{1,0:T(8,128)} copy(f32[64,128]{1,0:T(8,128)S(1)} %get-tuple-element.8) | data formatting | bytes 65536
  59.0 0.6 copy.25
  59.6 0.5 copy.26
  60.1 0.6 %copy.27 = f32[64,128]{1,0:T(8,128)} copy(f32[64,128]{1,0:T(8,128)S(1)} %get-tuple-element.11) | data formatting | bytes 65536
Async XLA Ops:
  1.9 1.6 %copy-start = (bf16[1,64,128,128]{3,2,1,0:T(8,128)(2,1)S(1)}, bf16[1,64,128,128]{3,2,1,0:T(8,128)(2,1)}, u32[]{:S(2)}) copy-start(bf16[1,64,128,128]{3,2,1,0:T(8,128)(2,1)} %tiles.1) | copy-start | bytes 6291460
  3.5 1.6 %copy-start.1 = (bf16[1,64,128,128]{3,2,1,0:T(8,128)(2,1)S(1)}, bf16[1,64,128,128]{3,2,1,0:T(8,128)(2,1)}, u32[]{:S(2)}) copy-start(bf16[1,64,128,128]{3,2,1,0:T(8,128)(2,1)} %cuts.1) | copy-start | bytes 6291460
  5.1 0.8 %copy-start.2 = (f32[64,128]{1,0:T(8,128)S(1)}, f32[64,128]{1,0:T(8,128)}, u32[]{:S(2)}) copy-start(f32[64,128]{1,0:T(8,128)} %cost.1) | copy-start | bytes 98308
  5.9 0.8 %copy-start.3 = (f32[64,128]{1,0:T(8,128)S(1)}, f32[64,128]{1,0:T(8,128)}, u32[]{:S(2)}) copy-start(f32[64,128]{1,0:T(8,128)} %x0.1) | copy-start | bytes 98308
  6.6 0.7 %copy-start.4 = (f32[32,128]{1,0:T(8,128)S(1)}, f32[32,128]{1,0:T(8,128)}, u32[]{:S(2)}) copy-start(f32[32,128]{1,0:T(8,128)} %demand.1) | copy-start | bytes 49156
  7.3 0.7 %copy-start.5 = (f32[32,128]{1,0:T(8,128)S(1)}, f32[32,128]{1,0:T(8,128)}, u32[]{:S(2)}) copy-start(f32[32,128]{1,0:T(8,128)} %y0.1) | copy-start | bytes 49156
  8.1 0.7 %copy-start.6 = (s32[1,64]{1,0:T(1,128)S(1)}, s32[1,64]{1,0:T(1,128)}, u32[]{:S(2)}) copy-start(s32[1,64]{1,0:T(1,128)} %row_of.1) | copy-start | bytes 772
  8.7 0.7 %copy-start.7 = (s32[1,64]{1,0:T(1,128)S(1)}, s32[1,64]{1,0:T(1,128)}, u32[]{:S(2)}) copy-start(s32[1,64]{1,0:T(1,128)} %col_of.1) | copy-start | bytes 772
  9.4 0.7 %copy-start.8 = (s32[1,64,1]{1,2,0:T(1,128)S(1)}, s32[1,64,1]{1,2,0:T(1,128)}, u32[]{:S(2)}) copy-start(s32[1,64,1]{1,2,0:T(1,128)} %param.18) | copy-start | bytes 772
  10.0 0.7 %copy-start.9 = (s32[1,64]{1,0:T(1,128)S(1)}, s32[1,64]{1,0:T(1,128)}, u32[]{:S(2)}) copy-start(s32[1,64]{1,0:T(1,128)} %cut_col.1) | copy-start | bytes 772
  10.7 0.7 %copy-start.10 = (f32[1,128]{1,0:T(1,128)S(1)}, f32[1,128]{1,0:T(1,128)}, u32[]{:S(2)}) copy-start(f32[1,128]{1,0:T(1,128)} %w0.1) | copy-start | bytes 1540
  11.3 0.7 %copy-start.11 = (s32[64]{0:T(128)S(1)}, s32[64]{0:T(128)}, u32[]{:S(2)}) copy-start(s32[64]{0:T(128)} %param.27) | copy-start | bytes 772

commit v2 on v1

--- a/solution.py
+++ b/solution.py
@@ -36,20 +36,20 @@
 def kernel(
     owners,
     n_row,
-    tiles,
-    row_of,
-    col_of,
-    cuts,
-    dest,
-    cut_col,
-    cost,
-    demand,
-    x0,
-    y0,
-    w0,
+    far_dest,
+    far_cut_col,
+    far_w0,
+    far_cuts,
+    far_row_of,
+    far_y0,
+    far_tiles,
+    far_col_of,
+    far_x0,
+    far_cost,
+    far_demand,
+    far_exps,
     weight,
     step,
-    exps,
     x_out,
     y_out,
     w_out,
@@ -62,11 +62,30 @@
     recv_p,
     send_r,
     recv_r,
+    dest,
+    cut_col,
+    w0,
+    cuts,
+    row_of,
+    y0,
+    tiles,
+    col_of,
+    x0,
+    cost,
+    demand,
+    exps,
+    sem_in,
     sem_a,
     sem_x,
     sem_p,
     sem_r,
 ):
+    far = (far_dest, far_cut_col, far_w0, far_cuts, far_row_of, far_y0)
+    far += (far_tiles, far_col_of, far_x0, far_cost, far_demand, far_exps)
+    near = (dest, cut_col, w0, cuts, row_of, y0, tiles, col_of, x0, cost, demand, exps)
+    loads = [pltpu.make_async_copy(a, b, sem_in.at[i]) for i, (a, b) in enumerate(zip(far, near))]
+    for load in loads:
+        load.start()
     c = lax.axis_index("col")
     r = lax.axis_index("row")
     n_dev = owners * n_row
@@ -90,13 +109,14 @@
 
     lax.fori_loop(1, n_dev, greet, 0)
 
+    for load in loads[:4]:
+        load.wait()
+
     def one_hot(row, size):
         return jnp.where(
             lax.broadcasted_iota(jnp.int32, (size, row.shape[1]), 0) == row, 1.0, 0.0
         )
 
-    row_table = one_hot(row_of[...], row_blocks).astype(BF)
-    col_table = one_hot(col_of[...], blocks).astype(BF)
     owner_table = one_hot(dest[...], max(owners, 16)).astype(BF)
     same = dot(owner_table, owner_table, (0, 0))
     earlier = lax.broadcasted_iota(jnp.int32, same.shape, 0) < lax.broadcasted_iota(
@@ -123,9 +143,11 @@
         parts = []
         for g in range(count // GROUP):
             rows = vectors[g * GROUP : (g + 1) * GROUP]
+            block = ref[0, g * GROUP : (g + 1) * GROUP].reshape(GROUP * width, width)
+            every = dot(rows, block, (1, 1))
             total = jnp.zeros((GROUP, width), F32)
             for k in range(GROUP):
-                total = total + dot(rows * masks[k], ref[0, g * GROUP + k], (1, 1))
+                total = jnp.where(line == k, every[:, k * width : (k + 1) * width], total)
             parts.append(total)
         return jnp.concatenate(parts, axis=0)
 
@@ -141,6 +163,8 @@
         )
         send_a[turn, :, STRIDE:] = stats
         recv_a[turn, flat] = send_a[turn, c]
+        if turn == 0:
+            pl.semaphore_wait(barrier, n_dev - 1)
 
         def go(k, carry):
             other = lax.rem(flat + k, n_dev)
@@ -192,9 +216,13 @@
 
         lax.fori_loop(1, owners, go, 0)
 
-    x, y, w = x0[...], y0[...], w0[...]
-    pl.semaphore_wait(barrier, n_dev - 1)
+    w = w0[...]
     send_cut(0, w, chosen.reshape(owners, STRIDE, width))
+    for load in loads[4:]:
+        load.wait()
+    row_table = one_hot(row_of[...], row_blocks).astype(BF)
+    col_table = one_hot(col_of[...], blocks).astype(BF)
+    x, y = x0[...], y0[...]
     send_rows(0, y, jnp.zeros((STRIDE, width), F32))
 
     eta = jnp.full((1, 1), step[0], F32)
@@ -304,6 +332,20 @@
     phases = ITERS + 1
     vmem = pl.BlockSpec(memory_space=pltpu.VMEM)
     smem = pl.BlockSpec(memory_space=pltpu.SMEM)
+    operands = (
+        cut_dest.reshape(cut_cols.shape),
+        cut_cols,
+        cut_start,
+        cut_tiles,
+        tile_row_blocks,
+        initial_duals,
+        covering_tiles,
+        tile_cols,
+        primal_start,
+        cost,
+        demand,
+        exponents.reshape(1, blocks),
+    )
     return pl.pallas_call(
         functools.partial(kernel, owners, n_row),
         out_shape=(
@@ -312,7 +354,7 @@
             jax.ShapeDtypeStruct(cut_start.shape, F32),
             jax.ShapeDtypeStruct(cost.shape, F32),
         ),
-        in_specs=[vmem] * 11 + [smem] * 2 + [vmem],
+        in_specs=[pl.BlockSpec(memory_space=pltpu.HBM)] * 12 + [smem] * 2,
         out_specs=(vmem,) * 4,
         scratch_shapes=[
             pltpu.VMEM((phases, owners, 2 * STRIDE, width), F32),
@@ -323,6 +365,8 @@
             pltpu.VMEM((ITERS, owners, row_blocks, width), F32),
             pltpu.VMEM((phases, blocks + STRIDE, width), F32),
             pltpu.VMEM((phases, n_row, blocks + STRIDE, width), F32),
+            *[pltpu.VMEM(a.shape, a.dtype) for a in operands],
+            pltpu.SemaphoreType.DMA((len(operands),)),
             pltpu.SemaphoreType.DMA((2, phases)),
             pltpu.SemaphoreType.DMA((2, ITERS)),
             pltpu.SemaphoreType.DMA((2, ITERS)),
@@ -332,22 +376,7 @@
             collective_id=0, has_side_effects=True, vmem_limit_bytes=44 * 1024 * 1024
         ),
         name="pdhg",
-    )(
-        covering_tiles,
-        tile_row_blocks,
-        tile_cols,
-        cut_tiles,
-        cut_dest.reshape(cut_cols.shape),
-        cut_cols,
-        cost,
-        demand,
-        primal_start,
-        initial_duals,
-        cut_start,
-        primal_weight,
-        step_size,
-        exponents.reshape(1, blocks),
-    )
+    )(*operands, primal_weight, step_size)
 
 
 def solution(mesh):

time: 61.2 us -> 60.6 us (level)
    pallas_call x1, Pallas kernels: 46.3 us -> 45.7 us  [local(): pl.pallas_call(functools.partial(kernel, owners, n_row), out_shape=(jax.S...]
where the time goes in v2:
time: 60.6 us; the launch traced here: 60.1 us
  Pallas kernels  45.7 us (75%)
  local copies, waits for them, and re-layouts  12.4 us (20%)
  between operations  1.96 us (3%)
    pallas_call x1, Pallas kernels, local(): pl.pallas_call(functools.partial(kernel, owners, n_row), out_shape=(jax.S...  45.7 us
    unnamed x28, local copies, waits for them, and re-layouts  12.4 us

profile of v2, /device:TPU:0, one launch (start us, length us, event | category | flops | bytes accessed | tf_op | source)
XLA Modules:
  0.0 60.1 jit_solution(15653249084728895291)
XLA Ops:
  1.9 0.0 copy-start
  1.9 1.6 %copy-done = bf16[1,64,128,128]{3,2,1,0:T(8,128)(2,1)S(1)} copy-done((bf16[1,64,128,128]{3,2,1,0:T(8,128)(2,1)S(1)}, bf16[1,64,128,128]{3,2,1,0:T(8,128)(2,1)}, u32[]{:S(2)}) %copy-start) | copy-done | bytes 2097176
  3.5 0.0 copy-start.1
  3.5 1.6 %copy-done.1 = bf16[1,64,128,128]{3,2,1,0:T(8,128)(2,1)S(1)} copy-done((bf16[1,64,128,128]{3,2,1,0:T(8,128)(2,1)S(1)}, bf16[1,64,128,128]{3,2,1,0:T(8,128)(2,1)}, u32[]{:S(2)}) %copy-start.1) | copy-done | bytes 2097176
  5.1 0.0 copy-start.2
  5.1 0.8 %copy-done.2 = f32[64,128]{1,0:T(8,128)S(1)} copy-done((f32[64,128]{1,0:T(8,128)S(1)}, f32[64,128]{1,0:T(8,128)}, u32[]{:S(2)}) %copy-start.2) | copy-done | bytes 32792
  5.9 0.0 copy-start.3
  5.9 0.8 %copy-done.3 = f32[64,128]{1,0:T(8,128)S(1)} copy-done((f32[64,128]{1,0:T(8,128)S(1)}, f32[64,128]{1,0:T(8,128)}, u32[]{:S(2)}) %copy-start.3) | copy-done | bytes 32792
  6.6 0.0 copy-start.4
  6.6 0.7 %copy-done.4 = f32[32,128]{1,0:T(8,128)S(1)} copy-done((f32[32,128]{1,0:T(8,128)S(1)}, f32[32,128]{1,0:T(8,128)}, u32[]{:S(2)}) %copy-start.4) | copy-done | bytes 16408
  7.3 0.0 copy-start.5
  7.3 0.7 %copy-done.5 = f32[32,128]{1,0:T(8,128)S(1)} copy-done((f32[32,128]{1,0:T(8,128)S(1)}, f32[32,128]{1,0:T(8,128)}, u32[]{:S(2)}) %copy-start.5) | copy-done | bytes 16408
  8.1 0.0 copy-start.6
  8.1 0.7 %copy-done.6 = s32[1,64,1]{1,2,0:T(1,128)S(1)} copy-done((s32[1,64,1]{1,2,0:T(1,128)S(1)}, s32[1,64,1]{1,2,0:T(1,128)}, u32[]{:S(2)}) %copy-start.6) | copy-done | bytes 280
  8.7 0.0 copy-start.7
  8.7 0.7 %copy-done.7 = s32[1,64]{1,0:T(1,128)S(1)} copy-done((s32[1,64]{1,0:T(1,128)S(1)}, s32[1,64]{1,0:T(1,128)}, u32[]{:S(2)}) %copy-start.7) | copy-done | bytes 280
  9.4 0.0 copy-start.8
  9.4 0.7 %copy-done.8 = f32[1,128]{1,0:T(1,128)S(1)} copy-done((f32[1,128]{1,0:T(1,128)S(1)}, f32[1,128]{1,0:T(1,128)}, u32[]{:S(2)}) %copy-start.8) | copy-done | bytes 536
  10.0 0.0 copy-start.9
  10.0 0.7 %copy-done.9 = s32[1,64]{1,0:T(1,128)S(1)} copy-done((s32[1,64]{1,0:T(1,128)S(1)}, s32[1,64]{1,0:T(1,128)}, u32[]{:S(2)}) %copy-start.9) | copy-done | bytes 280
  10.7 0.0 copy-start.10
  10.7 0.7 %copy-done.10 = s32[1,64]{1,0:T(1,128)S(1)} copy-done((s32[1,64]{1,0:T(1,128)S(1)}, s32[1,64]{1,0:T(1,128)}, u32[]{:S(2)}) %copy-start.10) | copy-done | bytes 280
  11.3 0.0 copy-start.11
  11.3 0.7 %copy-done.11 = s32[64]{0:T(128)S(1)} copy-done((s32[64]{0:T(128)S(1)}, s32[64]{0:T(128)}, u32[]{:S(2)}) %copy-start.11) | copy-done | bytes 280
  12.0 45.7 %pdhg.1 = (f32[64,128]{1,0:T(8,128)S(1)}, f32[32,128]{1,0:T(8,128)S(1)}, f32[1,128]{1,0:T(1,128)S(1)}, f32[64,128]{1,0:T(8,128)S(1)}) custom-call(s32[1,64]{1,0:T(1,128)S(1)} %bitcast.2, s32[1,64]{1,0:T(1,128)S(1)} %copy-done.7, f32[1,128]{1,0:T(1,128)S(1)} %copy-done.8, bf16[1,64,128,128]{3,2,1,0:T(8,128)(2,1)S(1)} %copy-done, s32[1,64]{1,0:T(1,128)S(1)} %copy-done.9, ...), custom_call_target="tpu_custom_call" | custom-call | tf_op jit(solution)/shard_map/pdhg/pallas_call | solution.py:349
  57.7 0.6 %copy.24 = f32[64,128]{1,0:T(8,128)} copy(f32[64,128]{1,0:T(8,128)S(1)} %get-tuple-element.8) | data formatting | bytes 65536
  58.3 0.6 %copy.25 = f32[32,128]{1,0:T(8,128)} copy(f32[32,128]{1,0:T(8,128)S(1)} %get-tuple-element.9) | data formatting | bytes 32768
  58.9 0.5 copy.26
  59.5 0.6 %copy.27 = f32[64,128]{1,0:T(8,128)} copy(f32[64,128]{1,0:T(8,128)S(1)} %get-tuple-element.11) | data formatting | bytes 65536
Async XLA Ops:
  1.9 1.6 %copy-start = (bf16[1,64,128,128]{3,2,1,0:T(8,128)(2,1)S(1)}, bf16[1,64,128,128]{3,2,1,0:T(8,128)(2,1)}, u32[]{:S(2)}) copy-start(bf16[1,64,128,128]{3,2,1,0:T(8,128)(2,1)} %far_cuts.1) | copy-start | bytes 6291460
  3.5 1.6 %copy-start.1 = (bf16[1,64,128,128]{3,2,1,0:T(8,128)(2,1)S(1)}, bf16[1,64,128,128]{3,2,1,0:T(8,128)(2,1)}, u32[]{:S(2)}) copy-start(bf16[1,64,128,128]{3,2,1,0:T(8,128)(2,1)} %far_tiles.1) | copy-start | bytes 6291460
  5.1 0.8 %copy-start.2 = (f32[64,128]{1,0:T(8,128)S(1)}, f32[64,128]{1,0:T(8,128)}, u32[]{:S(2)}) copy-start(f32[64,128]{1,0:T(8,128)} %far_x0.1) | copy-start | bytes 98308
  5.9 0.8 %copy-start.3 = (f32[64,128]{1,0:T(8,128)S(1)}, f32[64,128]{1,0:T(8,128)}, u32[]{:S(2)}) copy-start(f32[64,128]{1,0:T(8,128)} %far_cost.1) | copy-start | bytes 98308
  6.6 0.7 %copy-start.4 = (f32[32,128]{1,0:T(8,128)S(1)}, f32[32,128]{1,0:T(8,128)}, u32[]{:S(2)}) copy-start(f32[32,128]{1,0:T(8,128)} %far_y0.1) | copy-start | bytes 49156
  7.3 0.7 %copy-start.5 = (f32[32,128]{1,0:T(8,128)S(1)}, f32[32,128]{1,0:T(8,128)}, u32[]{:S(2)}) copy-start(f32[32,128]{1,0:T(8,128)} %far_demand.1) | copy-start | bytes 49156
  8.1 0.7 %copy-start.6 = (s32[1,64,1]{1,2,0:T(1,128)S(1)}, s32[1,64,1]{1,2,0:T(1,128)}, u32[]{:S(2)}) copy-start(s32[1,64,1]{1,2,0:T(1,128)} %param.18) | copy-start | bytes 772
  8.7 0.7 %copy-start.7 = (s32[1,64]{1,0:T(1,128)S(1)}, s32[1,64]{1,0:T(1,128)}, u32[]{:S(2)}) copy-start(s32[1,64]{1,0:T(1,128)} %far_cut_col.1) | copy-start | bytes 772
  9.4 0.7 %copy-start.8 = (f32[1,128]{1,0:T(1,128)S(1)}, f32[1,128]{1,0:T(1,128)}, u32[]{:S(2)}) copy-start(f32[1,128]{1,0:T(1,128)} %far_w0.1) | copy-start | bytes 1540
  10.0 0.7 %copy-start.9 = (s32[1,64]{1,0:T(1,128)S(1)}, s32[1,64]{1,0:T(1,128)}, u32[]{:S(2)}) copy-start(s32[1,64]{1,0:T(1,128)} %far_row_of.1) | copy-start | bytes 772
  10.7 0.7 %copy-start.10 = (s32[1,64]{1,0:T(1,128)S(1)}, s32[1,64]{1,0:T(1,128)}, u32[]{:S(2)}) copy-start(s32[1,64]{1,0:T(1,128)} %far_col_of.1) | copy-start | bytes 772
  11.3 0.7 %copy-start.11 = (s32[64]{0:T(128)S(1)}, s32[64]{0:T(128)}, u32[]{:S(2)}) copy-start(s32[64]{0:T(128)} %param.27) | copy-start | bytes 772

commit v3 on v2

--- a/solution.py
+++ b/solution.py
@@ -158,10 +158,10 @@
     def send_cut(turn, w, stats):
         wb = jnp.broadcast_to(w, (GROUP, width)).astype(BF)
         products = forward(cuts, lambda g: wb)
-        send_a[turn, :, :STRIDE] = spread(slot_table, products, (1, 0)).reshape(
-            owners, STRIDE, width
-        )
-        send_a[turn, :, STRIDE:] = stats
+        placed = spread(slot_table, products, (1, 0)).reshape(owners, STRIDE, width)
+        if stats is None:
+            stats = placed - placed.astype(BF).astype(F32)
+        send_a[turn] = jnp.concatenate([placed, stats], axis=1).astype(BF)
         recv_a[turn, flat] = send_a[turn, c]
         if turn == 0:
             pl.semaphore_wait(barrier, n_dev - 1)
@@ -230,20 +230,27 @@
     held = None
     for turn in range(ITERS + 1):
         wait_all(recv_a.at[turn], n_dev - 1, sem_a.at[1, turn])
+        landed = recv_a[turn].astype(F32)
+        prices = landed[:, :STRIDE].reshape(n_dev * STRIDE, width).astype(BF)
+        beside = landed[:, STRIDE:]
         if turn == 0:
-            held = recv_a[0, :, STRIDE:].reshape(n_dev * STRIDE, width).astype(BF)
-        prices = recv_a[turn, :, :STRIDE].reshape(n_dev * STRIDE, width)
-        cut_part = spread(held, prices, (0, 0))[:blocks]
+            held = beside.reshape(n_dev * STRIDE, width).astype(BF)
+        cut_part = dot(held, prices, (0, 0))
+        if turn == ITERS:
+            low = beside.reshape(n_dev * STRIDE, width).astype(BF)
+            cut_part = cut_part + dot(held, low, (0, 0))
+        cut_part = cut_part[:blocks]
         wait_all(recv_r.at[turn], n_row - 1, sem_r.at[1, turn])
         from_rows = recv_r[turn, 0]
         for other in range(1, n_row):
             from_rows = from_rows + recv_r[turn, other]
         grad = cost[...] + (cut_part - from_rows[:blocks])
         if turn == 1:
-            stats = jnp.sum(recv_a[turn, :, STRIDE:], axis=0)
-            moved = jnp.sum(stats[:1], axis=1, keepdims=True)
+            stats = jnp.sum(beside, axis=0)
+            moved = jnp.sum(stats[0:1] + stats[1:2] + stats[2:3], axis=1, keepdims=True)
             dual_moved = jnp.sum(
-                stats[1:2] + jnp.sum(from_rows[blocks:], axis=0, keepdims=True),
+                (stats[3:4] + stats[4:5] + stats[5:6])
+                + jnp.sum(from_rows[blocks:], axis=0, keepdims=True),
                 axis=1,
                 keepdims=True,
             )
@@ -256,14 +263,17 @@
         xbar = (2.0 * new_x - x).astype(BF)
 
         mine = (
-            recv_a[0, pl.ds(r * owners, owners), STRIDE:].reshape(slots, width)[:, :blocks].astype(BF)
+            recv_a[0, pl.ds(r * owners, owners)]
+            .astype(F32)[:, STRIDE:]
+            .reshape(slots, width)[:, :blocks]
+            .astype(BF)
         )
         send_x[turn] = dot(mine, xbar, (1, 0)).reshape(owners, STRIDE, width)
         recv_x[turn, c] = send_x[turn, c]
         to_columns(lambda oc: send_x.at[turn, oc], recv_x, sem_x, turn)
 
         xg = dot(col_table, xbar, (0, 0)).astype(BF)
-        send_p[turn] = spread(row_table, backward(tiles, xg), (1, 0))
+        send_p[turn] = spread(row_table, backward(tiles, xg), (1, 0)).astype(BF)
         recv_p[turn, c] = send_p[turn]
         to_columns(lambda oc: send_p.at[turn], recv_p, sem_p, turn)
 
@@ -275,15 +285,17 @@
         place = lax.broadcasted_iota(jnp.int32, (STRIDE, width), 0)
         step_x = jnp.where(r == 0, 1.0, 0.0) * (new_x - x)
         step_w = new_w - w
-        stats = jnp.where(
-            place == 0,
-            jnp.sum(step_x * step_x, axis=0, keepdims=True),
-            jnp.where(place == 1, step_w * step_w, 0.0),
-        )
-        send_cut(turn + 1, new_w, jnp.broadcast_to(stats[None], (owners, STRIDE, width)))
+        stats = None
+        if turn + 1 < ITERS:
+            pieces = split3(jnp.sum(step_x * step_x, axis=0, keepdims=True)) + split3(step_w * step_w)
+            stats = jnp.zeros((STRIDE, width), F32)
+            for at, piece in enumerate(pieces):
+                stats = jnp.where(place == at, piece.astype(F32), stats)
+            stats = jnp.broadcast_to(stats[None], (owners, STRIDE, width))
+        send_cut(turn + 1, new_w, stats)
 
         wait_all(recv_p.at[turn], owners - 1, sem_p.at[1, turn])
-        total = jnp.sum(recv_p[turn], axis=0)
+        total = jnp.sum(recv_p[turn].astype(F32), axis=0)
         new_y = jnp.maximum(y + sigma * (demand[...] - total), 0.0)
         step_y = new_y - y
         squares = jnp.sum((step_y * step_y).reshape(row_blocks // STRIDE, STRIDE, width), axis=0)
@@ -357,12 +369,12 @@
         in_specs=[pl.BlockSpec(memory_space=pltpu.HBM)] * 12 + [smem] * 2,
         out_specs=(vmem,) * 4,
         scratch_shapes=[
-            pltpu.VMEM((phases, owners, 2 * STRIDE, width), F32),
-            pltpu.VMEM((phases, n_dev, 2 * STRIDE, width), F32),
+            pltpu.VMEM((phases, owners, 2 * STRIDE, width), BF),
+            pltpu.VMEM((phases, n_dev, 2 * STRIDE, width), BF),
             pltpu.VMEM((ITERS, owners, STRIDE, width), F32),
             pltpu.VMEM((ITERS, owners, STRIDE, width), F32),
-            pltpu.VMEM((ITERS, row_blocks, width), F32),
-            pltpu.VMEM((ITERS, owners, row_blocks, width), F32),
+            pltpu.VMEM((ITERS, row_blocks, width), BF),
+            pltpu.VMEM((ITERS, owners, row_blocks, width), BF),
             pltpu.VMEM((phases, blocks + STRIDE, width), F32),
             pltpu.VMEM((phases, n_row, blocks + STRIDE, width), F32),
             *[pltpu.VMEM(a.shape, a.dtype) for a in operands],
@@ -373,7 +385,7 @@
             pltpu.SemaphoreType.DMA((2, phases)),
         ],
         compiler_params=pltpu.CompilerParams(
-            collective_id=0, has_side_effects=True, vmem_limit_bytes=44 * 1024 * 1024
+            collective_id=0, has_side_effects=True, vmem_limit_bytes=64 * 1024 * 1024
         ),
         name="pdhg",
     )(*operands, primal_weight, step_size)

time: 60.6 us -> 43.7 us (0.72)
  Pallas kernels: 45.7 us -> 36.2 us
  local copies, waits for them, and re-layouts: 12.4 us -> 5.18 us
    pallas_call x1, Pallas kernels: 45.7 us -> 36.2 us  [local(): pl.pallas_call(functools.partial(kernel, owners, n_row), out_shape=(jax.S...]
    unnamed x28 -> x4, local copies, waits for them, and re-layouts: 12.4 us -> 5.18 us
where the time goes in v3:
time: 43.7 us; the launch traced here: 43.3 us
  Pallas kernels  36.2 us (83%)
  local copies, waits for them, and re-layouts  5.18 us (12%)
  between operations  1.94 us (4%)
    pallas_call x1, Pallas kernels, local(): pl.pallas_call(functools.partial(kernel, owners, n_row), out_shape=(jax.S...  36.2 us
    unnamed x4, local copies, waits for them, and re-layouts  5.18 us

profile of v3, /device:TPU:0, one launch (start us, length us, event | category | flops | bytes accessed | tf_op | source)
XLA Modules:
  0.0 43.3 jit_solution(15298413555578660875)
XLA Ops:
  1.9 36.2 %pdhg.1 = (f32[64,128]{1,0:T(8,128)}, f32[32,128]{1,0:T(8,128)}, f32[1,128]{1,0:T(1,128)}, f32[64,128]{1,0:T(8,128)}) custom-call(s32[1,64]{1,0:T(1,128)} %bitcast.2, s32[1,64]{1,0:T(1,128)} %far_cut_col.1, f32[1,128]{1,0:T(1,128)} %far_w0.1, bf16[1,64,128,128]{3,2,1,0:T(8,128)(2,1)} %far_cuts.1, s32[1,64]{1,0:T(1,128)} %far_row_of.1, f32[32,128]{1,0:T(8,128)} %far_y0.1, ...), custom_call_target="tpu_custom_call" | custom-call | tf_op jit(solution)/shard_map/pdhg/pallas_call | solution.py:361
  38.2 1.4 %copy.24 = f32[64,128]{1,0:T(8,128)} copy(f32[64,128]{1,0:T(8,128)} %get-tuple-element.8) | data formatting | bytes 65536
  39.5 1.3 %copy.25 = f32[32,128]{1,0:T(8,128)} copy(f32[32,128]{1,0:T(8,128)} %get-tuple-element.9) | data formatting | bytes 32768
  40.9 1.1 %copy.26 = f32[1,128]{1,0:T(1,128)} copy(f32[1,128]{1,0:T(1,128)} %get-tuple-element.10) | data formatting | bytes 1024
  42.0 1.4 %copy.27 = f32[64,128]{1,0:T(8,128)} copy(f32[64,128]{1,0:T(8,128)} %get-tuple-element.11) | data formatting | bytes 65536

commit v4 on v3

--- a/solution.py
+++ b/solution.py
@@ -320,6 +320,15 @@
             wait_all(recv_p.at[turn], owners - 1, sem_p.at[0, turn])
 
 
+def hand_out(*refs):
+    sem = refs[8]
+    copies = [pltpu.make_async_copy(refs[i], refs[4 + i], sem.at[i]) for i in range(4)]
+    for copy in copies:
+        copy.start()
+    for copy in copies:
+        copy.wait()
+
+
 def local(
     covering_tiles,
     tile_row_blocks,
@@ -358,7 +367,7 @@
         demand,
         exponents.reshape(1, blocks),
     )
-    return pl.pallas_call(
+    results = pl.pallas_call(
         functools.partial(kernel, owners, n_row),
         out_shape=(
             jax.ShapeDtypeStruct(primal_start.shape, F32),
@@ -389,6 +398,16 @@
         ),
         name="pdhg",
     )(*operands, primal_weight, step_size)
+    anywhere = pl.BlockSpec(memory_space=pl.ANY)
+    return pl.pallas_call(
+        hand_out,
+        out_shape=tuple(jax.ShapeDtypeStruct(a.shape, a.dtype) for a in results),
+        in_specs=[anywhere] * 4,
+        out_specs=(anywhere,) * 4,
+        scratch_shapes=[pltpu.SemaphoreType.DMA((4,))],
+        compiler_params=pltpu.CompilerParams(vmem_limit_bytes=64 * 1024 * 1024),
+        name="hand_out",
+    )(*results)
 
 
 def solution(mesh):

time: 43.7 us -> 41.9 us (0.959)
  local copies, waits for them, and re-layouts: 5.18 us -> 0 us
  Pallas kernels: 36.2 us -> 39.9 us
    unnamed x4 -> x0, local copies, waits for them, and re-layouts: 5.18 us -> none
    pallas_call x0 -> x1, Pallas kernels: none -> 3.64 us  [local(): pl.pallas_call(hand_out, out_shape=tuple((jax.ShapeDtypeStruct(a.shape, a...]
where the time goes in v4:
time: 41.9 us; the launch traced here: 41.8 us
  Pallas kernels  39.9 us (95%)
  between operations  1.94 us (5%)
    pallas_call x1, Pallas kernels, local(): pl.pallas_call(functools.partial(kernel, owners, n_row), out_shape=(jax.S...  36.2 us
    pallas_call x1, Pallas kernels, local(): pl.pallas_call(hand_out, out_shape=tuple((jax.ShapeDtypeStruct(a.shape, a...  3.64 us

profile of v4, /device:TPU:0, one launch (start us, length us, event | category | flops | bytes accessed | tf_op | source)
XLA Modules:
  0.0 41.8 jit_solution(16923733519454883751)
XLA Ops:
  1.9 36.2 %pdhg.1 = (f32[64,128]{1,0:T(8,128)}, f32[32,128]{1,0:T(8,128)}, f32[1,128]{1,0:T(1,128)}, f32[64,128]{1,0:T(8,128)}) custom-call(s32[1,64]{1,0:T(1,128)} %bitcast.2, s32[1,64]{1,0:T(1,128)} %far_cut_col.1, f32[1,128]{1,0:T(1,128)} %far_w0.1, bf16[1,64,128,128]{3,2,1,0:T(8,128)(2,1)} %far_cuts.1, s32[1,64]{1,0:T(1,128)} %far_row_of.1, f32[32,128]{1,0:T(8,128)} %far_y0.1, ...), custom_call_target="tpu_custom_call" | custom-call | tf_op jit(solution)/shard_map/pdhg/pallas_call | solution.py:370
  38.2 3.6 %hand_out.1 = (f32[64,128]{1,0:T(8,128)}, f32[32,128]{1,0:T(8,128)}, f32[1,128]{1,0:T(1,128)}, f32[64,128]{1,0:T(8,128)}) custom-call(f32[64,128]{1,0:T(8,128)} %get-tuple-element.8.refs_0_, f32[32,128]{1,0:T(8,128)} %get-tuple-element.9.refs_1_, f32[1,128]{1,0:T(1,128)} %get-tuple-element.10.refs_2_, f32[64,128]{1,0:T(8,128)} %get-tuple-element.11.refs_3_), custom_call_target="tpu_custom_call" | custom-call | tf_op jit(solution)/shard_map/hand_out/pallas_call | solution.py:402

commit v5 on v3

--- a/solution.py
+++ b/solution.py
@@ -320,6 +320,11 @@
             wait_all(recv_p.at[turn], owners - 1, sem_p.at[0, turn])
 
 
+def hand_out(*refs):
+    for source, target in zip(refs[:4], refs[4:]):
+        target[...] = source[...]
+
+
 def local(
     covering_tiles,
     tile_row_blocks,
@@ -358,7 +363,7 @@
         demand,
         exponents.reshape(1, blocks),
     )
-    return pl.pallas_call(
+    results = pl.pallas_call(
         functools.partial(kernel, owners, n_row),
         out_shape=(
             jax.ShapeDtypeStruct(primal_start.shape, F32),
@@ -389,6 +394,14 @@
         ),
         name="pdhg",
     )(*operands, primal_weight, step_size)
+    return pl.pallas_call(
+        hand_out,
+        out_shape=tuple(jax.ShapeDtypeStruct(a.shape, a.dtype) for a in results),
+        in_specs=[vmem] * 4,
+        out_specs=(vmem,) * 4,
+        compiler_params=pltpu.CompilerParams(vmem_limit_bytes=64 * 1024 * 1024),
+        name="hand_out",
+    )(*results)
 
 
 def solution(mesh):

time: 43.7 us -> 39.8 us (0.911)
  local copies, waits for them, and re-layouts: 5.18 us -> 0 us
  Pallas kernels: 36.2 us -> 37.7 us
    unnamed x4 -> x0, local copies, waits for them, and re-layouts: 5.18 us -> none
    pallas_call x0 -> x1, Pallas kernels: none -> 1.44 us  [local(): pl.pallas_call(hand_out, out_shape=tuple((jax.ShapeDtypeStruct(a.shape, a...]
where the time goes in v5:
time: 39.8 us; the launch traced here: 39.6 us
  Pallas kernels  37.7 us (95%)
  between operations  1.94 us (5%)
    pallas_call x1, Pallas kernels, local(): pl.pallas_call(functools.partial(kernel, owners, n_row), out_shape=(jax.S...  36.2 us
    pallas_call x1, Pallas kernels, local(): pl.pallas_call(hand_out, out_shape=tuple((jax.ShapeDtypeStruct(a.shape, a...  1.44 us

profile of v5, /device:TPU:0, one launch (start us, length us, event | category | flops | bytes accessed | tf_op | source)
XLA Modules:
  0.0 39.6 jit_solution(13248865629486305347)
XLA Ops:
  1.9 36.2 %pdhg.1 = (f32[64,128]{1,0:T(8,128)}, f32[32,128]{1,0:T(8,128)}, f32[1,128]{1,0:T(1,128)}, f32[64,128]{1,0:T(8,128)}) custom-call(s32[1,64]{1,0:T(1,128)} %bitcast.2, s32[1,64]{1,0:T(1,128)} %far_cut_col.1, f32[1,128]{1,0:T(1,128)} %far_w0.1, bf16[1,64,128,128]{3,2,1,0:T(8,128)(2,1)} %far_cuts.1, s32[1,64]{1,0:T(1,128)} %far_row_of.1, f32[32,128]{1,0:T(8,128)} %far_y0.1, ...), custom_call_target="tpu_custom_call" | custom-call | tf_op jit(solution)/shard_map/pdhg/pallas_call | solution.py:366
  38.2 1.4 %hand_out.1 = (f32[64,128]{1,0:T(8,128)}, f32[32,128]{1,0:T(8,128)}, f32[1,128]{1,0:T(1,128)}, f32[64,128]{1,0:T(8,128)}) custom-call(f32[64,128]{1,0:T(8,128)} %get-tuple-element.8.refs_0_, f32[32,128]{1,0:T(8,128)} %get-tuple-element.9.refs_1_, f32[1,128]{1,0:T(1,128)} %get-tuple-element.10.refs_2_, f32[64,128]{1,0:T(8,128)} %get-tuple-element.11.refs_3_), custom_call_target="tpu_custom_call" | custom-call | tf_op jit(solution)/shard_map/hand_out/pallas_call | solution.py:397
